TPU v7x, 32 devices: a whole 2x2x4 slice. The times are simulated.
32 devices in a mesh: vintage: 4 (over y, core), inline: 4 (over z), xline: 2 (over x).
Axes of the slice: x: 2, y: 2, z: 4, core: 2. Of those that a mesh axis runs over, the one named last changes fastest.
Arguments:
- amplitude: float32 [4, 32, 32, 256], P('vintage', 'inline', 'xline'), may hold values from -6 to 6
- inline_slope: int32 [4, 32, 32], P('vintage', 'inline', 'xline'), may hold values from -2 to 2
- crossline_slope: int32 [4, 32, 32], P('vintage', 'inline', 'xline'), may hold values from -2 to 2
Outputs:
- semblance: float32 [4, 32, 32, 256], P('vintage', 'inline', 'xline')
- lag_correl: float32 [4, 32, 32, 264], P('vintage', 'inline', 'xline')
All inputs are finite; a program needn't handle non-finite values.
Results may differ from a plain program's by a relative error of at most 0.0003.
Values sent between devices are 32-bit elements; how exact they have to be, the bound alone decides.
A program may use at most 64 MiB of HBM per device.

v0:
```python
import jax
import jax.numpy as jnp
from jax import lax
from jax.sharding import PartitionSpec as P

TIME_SAMPLES = 256
MAX_DIP_STEP = 2
RT = 4
LAGS = 33
NWIN = 8


EPS = 1e-06


def padded_2(block, sides, width):
    for axis, dim in sides:
        count = lax.axis_size(axis)
        forward = [(i, i + 1) for i in range(count - 1)]
        backward = [(target, source) for source, target in forward]
        low = lax.ppermute(
            lax.slice_in_dim(block, block.shape[dim] - width, None, axis=dim), axis, forward
        )
        high = lax.ppermute(lax.slice_in_dim(block, 0, width, axis=dim), axis, backward)
        block = jnp.concatenate([low, block, high], axis=dim)
    return block


def from_root(shard, axis, root):
    mine = lax.axis_index(axis) == root
    return lax.psum(jnp.where(mine, shard, jnp.zeros_like(shard)), axis)


def attribute_padded(padded, dip_il, dip_xl):
    inner_i = padded.shape[0] - 2
    inner_x = padded.shape[1] - 2
    padding = 2 * MAX_DIP_STEP + RT
    extent = TIME_SAMPLES + 2 * RT
    stack = jnp.zeros((inner_i, inner_x, extent), jnp.float32)
    power = jnp.zeros((inner_i, inner_x, extent), jnp.float32)
    for row_step in (-1, 0, 1):
        for col_step in (-1, 0, 1):
            neighbor = padded[
                1 + row_step : 1 + row_step + inner_i, 1 + col_step : 1 + col_step + inner_x, :
            ]
            shift_map = row_step * dip_il + col_step * dip_xl
            reach = (abs(row_step) + abs(col_step)) * MAX_DIP_STEP
            moved = jnp.zeros((inner_i, inner_x, extent), jnp.float32)
            for offset_value in range(-reach, reach + 1):
                start = padding - RT + offset_value
                shifted = neighbor[:, :, start : start + extent]
                moved = jnp.where((shift_map == offset_value)[:, :, None], shifted, moved)
            stack = stack + moved
            power = power + moved * moved
    numer = jnp.zeros((inner_i, inner_x, TIME_SAMPLES), jnp.float32)
    denom = jnp.zeros((inner_i, inner_x, TIME_SAMPLES), jnp.float32)
    for window_step in range(2 * RT + 1):
        piece = stack[:, :, window_step : window_step + TIME_SAMPLES]
        numer = numer + piece * piece
        denom = denom + power[:, :, window_step : window_step + TIME_SAMPLES]
    semb = numer / (9.0 * denom + EPS)
    attr = semb * stack[:, :, RT : RT + TIME_SAMPLES] / 9.0
    return (semb, attr)


def time_pad(volume):
    padding = 2 * MAX_DIP_STEP + RT
    return jnp.pad(volume, ((0, 0), (0, 0), (padding, padding)))


def correlate(monitor, baseline):
    half_lags = LAGS // 2
    inner_i, inner_x = (monitor.shape[0], monitor.shape[1])
    base_pad = jnp.pad(baseline, ((0, 0), (0, 0), (half_lags, half_lags)))
    mon_energy = jnp.sum(monitor * monitor, axis=-1)
    base_energy = jnp.sum(baseline * baseline, axis=-1)
    factor = NWIN / jnp.sqrt(mon_energy * base_energy + EPS)
    columns = []
    for lag_index in range(LAGS):
        product = monitor * base_pad[:, :, lag_index : lag_index + TIME_SAMPLES]
        columns.append(
            jnp.sum(product.reshape(inner_i, inner_x, NWIN, TIME_SAMPLES // NWIN), axis=-1)
        )
    result = jnp.stack(columns, axis=2) * factor[:, :, None, None]
    return result.reshape(inner_i, inner_x, LAGS * NWIN)


def per_device(amplitude, inline_slope, crossline_slope):
    volume = amplitude[0]
    dips_il = inline_slope[0]
    dips_xl = crossline_slope[0]
    rimmed = padded_2(volume, (("inline", 0), ("xline", 1)), 1)
    semb, attr = attribute_padded(time_pad(rimmed), dips_il, dips_xl)
    base_attr = from_root(attr, "vintage", 0)
    correl = correlate(attr, base_attr)
    return (semb[None], correl[None])


def solution(mesh):
    return jax.shard_map(
        per_device,
        mesh=mesh,
        in_specs=(
            P("vintage", "inline", "xline", None),
            P("vintage", "inline", "xline"),
            P("vintage", "inline", "xline"),
        ),
        out_specs=(P("vintage", "inline", "xline", None), P("vintage", "inline", "xline", None)),
        check_vma=False,
    )
```

profile of v0, /device:TPU:0, one launch (start us, length us, event | category | flops | bytes accessed | tf_op | source)
XLA Modules:
  0.0 139.5 jit_solution(18214201915103587438)
XLA Ops:
  8.0 4.9 %collective-permute-start = (f32[1,16,256]{2,1,0:T(8,128)S(1)}, f32[1,16,256]{2,1,0:T(8,128)S(1)}, u32[]{:S(2)}, u32[]{:S(2)}) collective-permute-start(f32[1,16,256]{2,1,0:T(8,128)S(1)} %get-tuple-element.64), channel_id=1, source_target_pairs={{0,2},{2,4},{4,6},{1,3},{3,5},{5,7},{8,10},{10,12},{12,14},{9,11},... | collective-permute-start | bytes 49160 | tf_op jit(solution)/shard_map/ppermute | solution.py:21
  12.9 1.3 collective-permute-start.1
  15.0 3.5 %collective-permute-done.1 = f32[1,16,256]{2,1,0:T(8,128)S(1)} collective-permute-done((f32[1,16,256]{2,1,0:T(8,128)S(1)}, f32[1,16,256]{2,1,0:T(8,128)S(1)}, u32[]{:S(2)}, u32[]{:S(2)}) %collective-permute-start.1) | collective-permute-done | bytes 16416 | tf_op jit(solution)/shard_map/ppermute | solution.py:24
  19.4 3.4 %collective-permute-start.2 = (f32[10,1,256]{2,1,0:T(1,128)S(1)}, f32[10,1,256]{2,1,0:T(1,128)S(1)}, u32[]{:S(2)}, u32[]{:S(2)}) collective-permute-start(f32[10,1,256]{2,1,0:T(1,128)S(1)} %get-tuple-element.61), channel_id=1, source_target_pairs={{0,1},{2,3},{4,5},{6,7},{8,9},{10,11},{12,13},{14,15},{16,17},{18,... | collective-permute-start | bytes 30728 | tf_op jit(solution)/shard_map/ppermute | solution.py:21
  22.8 1.3 collective-permute-start.3
  24.2 4.2 %collective-permute-done.3 = f32[10,1,256]{2,1,0:T(1,128)S(1)} collective-permute-done((f32[10,1,256]{2,1,0:T(1,128)S(1)}, f32[10,1,256]{2,1,0:T(1,128)S(1)}, u32[]{:S(2)}, u32[]{:S(2)}) %collective-permute-start.3) | collective-permute-done | bytes 10272 | tf_op jit(solution)/shard_map/ppermute | solution.py:24
  28.4 1.1 select_maximum_fusion
  29.5 4.3 %add_add_fusion = (f32[8,16,264]{2,1,0:T(8,128)S(1)}, f32[8,16,264]{2,1,0:T(8,128)S(1)}, f32[8,16,264]{2,1,0:T(8,128)S(1)}, f32[8,16,264]{2,1,0:T(8,128)S(1)}, f...) fusion(f32[10,18,272]{2,1,0:T(8,128)S(1)} %select_maximum_fusio, ...), kind=kLoop, calls=%fused_computation.97 | loop fusion | flops 2162688 | bytes 8928256 | tf_op jit(solution)/shard_map/add | solution.py:53
  34.0 1.3 multiply_reduce_fusion.1
  35.9 30.9 %all-reduce.4.cloned.1.call-done = f32[8,16,256]{2,1,0:T(8,128)} async-done(((f32[8,16,256]{2,1,0:T(8,128)}), f32[8,16,256]{2,1,0:T(8,128)}) %all-reduce.4.cloned.1.call-update) | async-done | bytes 131088 | tf_op jit(solution)/shard_map/psum | solution.py:31
  66.8 3.0 %fusion.63 = (f32[8,16,256]{2,1,0:T(8,128)S(1)}, f32[8,16,256]{2,1,0:T(8,128)S(1)}, f32[8,16,256]{2,1,0:T(8,128)S(1)}, f32[8,16,256]{2,1,0:T(8,128)S(1)}, f32[8,...) fusion(f32[8,16,256]{2,1,0:T(8,128)S(1)} %get-tuple-element.9, ...), kind=kLoop, calls=%fused_computation.112 | loop fusion | flops 556928 | bytes 2228736 | tf_op jit(solution)/shard_map/mul | solution.py:80
  83.6 1.8 %fusion.80 = (f32[8,16,256]{2,1,0:T(8,128)}, f32[8,16,256]{2,1,0:T(8,128)}, f32[8,16,256]{2,1,0:T(8,128)}, f32[8,16,256]{2,1,0:T(8,128)}, f32[8,16,256]{2,1,0:T(...) fusion(f32[8,16,256]{2,1,0:T(8,128)S(1)} %get-tuple-element.9, ...), kind=kLoop, calls=%fused_computation.129 | loop fusion | flops 589824 | bytes 2621440 | tf_op jit(solution)/shard_map/mul | solution.py:80
  85.3 1.1 reshape.509
  87.2 1.1 reshape.508
  89.1 1.1 reshape.507
  91.0 1.1 reshape.506
  92.9 1.1 reshape.505
  94.8 1.1 reshape.504
  96.7 1.1 reshape.503
  98.6 1.1 reshape.502
  100.5 1.1 reshape.501
  102.4 1.1 reshape.500
  104.3 1.1 reshape.499
  131.6 1.1 copy.42
  (128 shorter events, 51.2 us)
Async XLA Ops:
  7.2 59.6 %all-reduce.4.cloned.1.call-start = ((), (), s32[]{:S(2)}) async-start(), calls=%async_computation | async-start | bytes 262144 | tf_op jit(solution)/shard_map/psum | solution.py:31
  8.0 7.0 %collective-permute-start = (f32[1,16,256]{2,1,0:T(8,128)S(1)}, f32[1,16,256]{2,1,0:T(8,128)S(1)}, u32[]{:S(2)}, u32[]{:S(2)}) collective-permute-start(f32[1,16,256]{2,1,0:T(8,128)S(1)} %get-tuple-element.64), channel_id=1, source_target_pairs={{0,2},{2,4},{4,6},{1,3},{3,5},{5,7},{8,10},{10,12},{12,14},{9,11},... | collective-permute-start | bytes 49160 | tf_op jit(solution)/shard_map/ppermute | solution.py:21
  12.9 5.6 %collective-permute-start.1 = (f32[1,16,256]{2,1,0:T(8,128)S(1)}, f32[1,16,256]{2,1,0:T(8,128)S(1)}, u32[]{:S(2)}, u32[]{:S(2)}) collective-permute-start(f32[1,16,256]{2,1,0:T(8,128)S(1)} %get-tuple-element.65), channel_id=1, source_target_pairs={{2,0},{4,2},{6,4},{3,1},{5,3},{7,5},{10,8},{12,10},{14,12},{11,9},... | collective-permute-start | bytes 49160 | tf_op jit(solution)/shard_map/ppermute | solution.py:24
  19.4 4.8 %collective-permute-start.2 = (f32[10,1,256]{2,1,0:T(1,128)S(1)}, f32[10,1,256]{2,1,0:T(1,128)S(1)}, u32[]{:S(2)}, u32[]{:S(2)}) collective-permute-start(f32[10,1,256]{2,1,0:T(1,128)S(1)} %get-tuple-element.61), channel_id=1, source_target_pairs={{0,1},{2,3},{4,5},{6,7},{8,9},{10,11},{12,13},{14,15},{16,17},{18,... | collective-permute-start | bytes 30728 | tf_op jit(solution)/shard_map/ppermute | solution.py:21
  22.8 5.6 %collective-permute-start.3 = (f32[10,1,256]{2,1,0:T(1,128)S(1)}, f32[10,1,256]{2,1,0:T(1,128)S(1)}, u32[]{:S(2)}, u32[]{:S(2)}) collective-permute-start(f32[10,1,256]{2,1,0:T(1,128)S(1)} %get-tuple-element.62), channel_id=1, source_target_pairs={{1,0},{3,2},{5,4},{7,6},{9,8},{11,10},{13,12},{15,14},{17,16},{19,... | collective-permute-start | bytes 30728 | tf_op jit(solution)/shard_map/ppermute | solution.py:24
  80.3 3.2 %copy-start = (f32[8,16,256]{2,1,0:T(8,128)S(1)}, f32[8,16,256]{2,1,0:T(8,128)}, u32[]{:S(2)}) copy-start(f32[8,16,256]{2,1,0:T(8,128)} %all-reduce.4.cloned.1.call-done) | copy-start | bytes 393220
  111.3 8.9 %copy-start.8 = (f32[8,16,8]{2,1,0:T(8,128)S(1)}, f32[8,16,8]{2,1,0:T(8,128)}, u32[]{:S(2)}) copy-start(f32[8,16,8]{2,1,0:T(8,128)} %reduce_sum.323) | copy-start | bytes 12292
  111.3 8.9 %copy-start.6 = (f32[8,16,8]{2,1,0:T(8,128)S(1)}, f32[8,16,8]{2,1,0:T(8,128)}, u32[]{:S(2)}) copy-start(f32[8,16,8]{2,1,0:T(8,128)} %reduce_sum.324) | copy-start | bytes 12292
  111.3 8.9 %copy-start.4 = (f32[8,16,8]{2,1,0:T(8,128)S(1)}, f32[8,16,8]{2,1,0:T(8,128)}, u32[]{:S(2)}) copy-start(f32[8,16,8]{2,1,0:T(8,128)} %reduce_sum.325) | copy-start | bytes 12292
  111.3 8.9 %copy-start.3 = (f32[8,16,8]{2,1,0:T(8,128)S(1)}, f32[8,16,8]{2,1,0:T(8,128)}, u32[]{:S(2)}) copy-start(f32[8,16,8]{2,1,0:T(8,128)} %reduce_sum.326) | copy-start | bytes 12292
  111.4 8.9 %copy-start.2 = (f32[8,16,8]{2,1,0:T(8,128)S(1)}, f32[8,16,8]{2,1,0:T(8,128)}, u32[]{:S(2)}) copy-start(f32[8,16,8]{2,1,0:T(8,128)} %reduce_sum.327) | copy-start | bytes 12292
  112.2 8.1 %copy-start.1 = (f32[8,16,8]{2,1,0:T(8,128)S(1)}, f32[8,16,8]{2,1,0:T(8,128)}, u32[]{:S(2)}) copy-start(f32[8,16,8]{2,1,0:T(8,128)} %reduce_sum.328) | copy-start | bytes 12292
  113.4 17.1 %copy-start.12 = (f32[8,16,8]{2,1,0:T(8,128)S(1)}, f32[8,16,8]{2,1,0:T(8,128)}, u32[]{:S(2)}) copy-start(f32[8,16,8]{2,1,0:T(8,128)} %reduce_sum.342) | copy-start | bytes 12292
  113.4 17.1 %copy-start.11 = (f32[8,16,8]{2,1,0:T(8,128)S(1)}, f32[8,16,8]{2,1,0:T(8,128)}, u32[]{:S(2)}) copy-start(f32[8,16,8]{2,1,0:T(8,128)} %reduce_sum.343) | copy-start | bytes 12292
  113.4 17.1 %copy-start.10 = (f32[8,16,8]{2,1,0:T(8,128)S(1)}, f32[8,16,8]{2,1,0:T(8,128)}, u32[]{:S(2)}) copy-start(f32[8,16,8]{2,1,0:T(8,128)} %reduce_sum.344) | copy-start | bytes 12292
  113.4 17.2 %copy-start.9 = (f32[8,16,8]{2,1,0:T(8,128)S(1)}, f32[8,16,8]{2,1,0:T(8,128)}, u32[]{:S(2)}) copy-start(f32[8,16,8]{2,1,0:T(8,128)} %reduce_sum.345) | copy-start | bytes 12292
  113.4 17.2 %copy-start.7 = (f32[8,16,8]{2,1,0:T(8,128)S(1)}, f32[8,16,8]{2,1,0:T(8,128)}, u32[]{:S(2)}) copy-start(f32[8,16,8]{2,1,0:T(8,128)} %reduce_sum.346) | copy-start | bytes 12292
  114.2 16.3 %copy-start.5 = (f32[8,16,8]{2,1,0:T(8,128)S(1)}, f32[8,16,8]{2,1,0:T(8,128)}, u32[]{:S(2)}) copy-start(f32[8,16,8]{2,1,0:T(8,128)} %reduce_sum.347) | copy-start | bytes 12292
Sparse Core Ops, SparseCore 0:
  36.0 30.7 all-reduce.3
where the time goes:
time: 141 us; the launch traced here: 140 us
  other arithmetic  40.2 us (29%)
  waiting for transfers between devices  38.7 us (27%)
  local copies, waits for them, and re-layouts  35.2 us (25%)
  between operations  14.5 us (10%)
  starting transfers between devices  10.9 us (8%)
    psum x1, waiting for transfers between devices, from_root(): return lax.psum(jnp.where(mine, shard, jnp.zeros_like(shard)), axis)  30.9 us
    reduce_sum x33, other arithmetic, correlate(): jnp.sum(product.reshape(inner_i, inner_x, NWIN, TIME_SAMPLES // NWIN), ax...  26.2 us
    unnamed x59, local copies, waits for them, and re-layouts  17.3 us
    reshape x33, local copies, waits for them, and re-layouts, correlate(): product.reshape(inner_i, inner_x, NWIN, TIME_SAMPLES // NWIN)  16.2 us
    ppermute x2, starting transfers between devices, padded_2(): lax.ppermute(lax.slice_in_dim(block, block.shape[dim] - width, None, axis...  8.31 us
    ppermute x2, waiting for transfers between devices, padded_2(): lax.ppermute(lax.slice_in_dim(block, 0, width, axis=dim), axis, backward)  7.73 us
    mul x2, other arithmetic, correlate(): product = monitor * base_pad[:, :, lag_index:lag_index + TIME_SAMPLES]  4.74 us
    add x1, other arithmetic, attribute_padded(): stack = stack + moved  4.27 us
  transfers between devices with their start and end apart: 5, of which 3 were waited for; matrix products, arithmetic and copies ran while one was open for 1% of the time, Pallas kernels for 0%

commit v1 on v0

v1 whole, which is shorter than its diff:
```python
import functools

import jax
import jax.numpy as jnp
from jax import lax
from jax.experimental import pallas as pl
from jax.experimental.pallas import tpu as pltpu
from jax.sharding import PartitionSpec as P

TIME_SAMPLES = 256
MAX_DIP_STEP = 2
RT = 4
LAGS = 33
NWIN = 8
EPS = 1e-06

WIN = TIME_SAMPLES // NWIN
HALF = LAGS // 2
REACH = 2 * MAX_DIP_STEP
PAD = 8
CHUNK = 8
CHUNKS = WIN // CHUNK
MESH = pl.DeviceIdType.MESH
DIRECTIONS = [(a, b) for a in (-1, 0, 1) for b in (-1, 0, 1) if (a, b) != (0, 0)]
OFFSETS = [(a, b) for a in (-1, 0, 1) for b in (-1, 0, 1)]


def lane_dips(dips, rows, cols):
    lanes = rows * cols
    col = lax.broadcasted_iota(jnp.int32, (cols, lanes), 0)
    lane = lax.broadcasted_iota(jnp.int32, (cols, lanes), 1)
    spread = jnp.where(lane % cols == col, 1.0, 0.0).astype(jnp.float32)
    tiled = jnp.dot(dips.astype(jnp.float32), spread, preferred_element_type=jnp.float32)
    row = lax.broadcasted_iota(jnp.int32, (rows, lanes), 0)
    here = lax.broadcasted_iota(jnp.int32, (rows, lanes), 1) // cols == row
    return jnp.sum(jnp.where(here, tiled, 0.0), axis=0, keepdims=True)


def select_shift(rows, shift, reach):
    left = shift + float(reach)
    step = 8 if reach > 3 else 4
    while step:
        on = left >= float(step)
        left = jnp.where(on, left - float(step), left)
        count = len(rows) - step if step > 1 else CHUNK
        keep = min(count, len(rows))
        need = CHUNK + step - 1
        rows = [
            jnp.where(on, rows[k + step], rows[k]) if k + step < len(rows) else rows[k]
            for k in range(min(len(rows), need))
        ]
        step //= 2
    return rows[:CHUNK]


def kernel(
    rows, cols, vintages, inlines, xlines,
    amp, dip_il, dip_xl, semb_out, corr_out,
    tile, times, stack, power, attr, base, semb_t, semb_n, corr_t, corr_n, d_il, d_xl,
    load_sem, store_sem, halo_send, halo_recv, base_send, base_recv,
):
    v = lax.axis_index("vintage")
    i = lax.axis_index("inline")
    x = lax.axis_index("xline")
    loads = [
        pltpu.make_async_copy(amp.at[0], tile.at[pl.ds(1, rows), pl.ds(PAD, cols), :], load_sem.at[0]),
        pltpu.make_async_copy(dip_il.at[0], d_il, load_sem.at[1]),
        pltpu.make_async_copy(dip_xl.at[0], d_xl, load_sem.at[2]),
    ]
    for load in loads:
        load.start()

    edge = jnp.zeros((PAD, TIME_SAMPLES), jnp.float32)
    for row in range(rows + 2):
        tile[row, 0:PAD, :] = edge
        tile[row, PAD + cols : 2 * PAD + cols, :] = edge
    for row in (0, rows + 1):
        tile[row, PAD : PAD + cols, :] = jnp.zeros((cols, TIME_SAMPLES), jnp.float32)

    def inside(a, b):
        return (i + a >= 0) & (i + a < inlines) & (x + b >= 0) & (x + b < xlines)

    barrier = pltpu.get_barrier_semaphore()
    greeted = jnp.int32(0)
    for a, b in DIRECTIONS:
        there = inside(a, b)
        greeted = greeted + jnp.where(there, 1, 0)

        @pl.when(there)
        def _():
            pl.semaphore_signal(
                barrier, inc=1, device_id={"inline": i + a, "xline": x + b}, device_id_type=MESH
            )

    @pl.when(v != 0)
    def _():
        pl.semaphore_signal(barrier, inc=1, device_id={"vintage": 0}, device_id_type=MESH)

    greeted = greeted + jnp.where(v == 0, vintages - 1, 0)
    pl.semaphore_wait(barrier, greeted)

    def halo(index):
        a, b = DIRECTIONS[index]
        row_from = {-1: pl.ds(0, 1), 0: pl.ds(0, rows), 1: pl.ds(rows - 1, 1)}[a]
        row_to = {-1: pl.ds(rows + 1, 1), 0: pl.ds(1, rows), 1: pl.ds(0, 1)}[a]
        col_from = {-1: pl.ds(0, PAD), 0: pl.ds(0, cols), 1: pl.ds(cols - PAD, PAD)}[b]
        col_to = {-1: pl.ds(PAD + cols, PAD), 0: pl.ds(PAD, cols), 1: pl.ds(0, PAD)}[b]
        return pltpu.make_async_remote_copy(
            src_ref=amp.at[0, row_from, col_from, :],
            dst_ref=tile.at[row_to, col_to, :],
            send_sem=halo_send.at[index],
            recv_sem=halo_recv.at[index],
            device_id={"inline": i + a, "xline": x + b},
            device_id_type=MESH,
        )

    for index, (a, b) in enumerate(DIRECTIONS):

        @pl.when(inside(a, b))
        def _():
            halo(index).start()

    for load in loads:
        load.wait()
    dips = [lane_dips(d_il[...], rows, cols), lane_dips(d_xl[...], rows, cols)]
    lanes = rows * cols
    dips = [jnp.broadcast_to(dip, (NWIN, lanes)) for dip in dips]
    blank = jnp.zeros((PAD, lanes), jnp.float32)
    for slot in range(len(OFFSETS)):
        times[slot, 0:PAD, :] = blank
        times[slot, PAD + TIME_SAMPLES : 2 * PAD + TIME_SAMPLES, :] = blank

    for index, (a, b) in enumerate(DIRECTIONS):

        @pl.when(inside(-a, -b))
        def _():
            halo(index).wait_recv()

    for slot, (a, b) in enumerate(OFFSETS):
        block = tile[1 + a : 1 + a + rows, PAD + b : PAD + b + cols, :]
        times[slot, PAD : PAD + TIME_SAMPLES, :] = block.reshape(lanes, TIME_SAMPLES).T

    @pl.loop(0, CHUNKS + 1)
    def _(chunk):
        first = chunk * CHUNK
        total = [None] * CHUNK
        squares = [None] * CHUNK
        for slot, (a, b) in enumerate(OFFSETS):
            reach = (abs(a) + abs(b)) * MAX_DIP_STEP
            taps = [
                times[slot, pl.ds(first + REACH - reach + k, NWIN, stride=WIN), :]
                for k in range(CHUNK + 2 * reach)
            ]
            moved = taps
            if reach:
                moved = select_shift(taps, float(a) * dips[0] + float(b) * dips[1], reach)
            for k in range(CHUNK):
                square = moved[k] * moved[k]
                total[k] = moved[k] if total[k] is None else total[k] + moved[k]
                squares[k] = square if squares[k] is None else squares[k] + square
        for k in range(CHUNK):
            stack[first + k] = total[k]
            power[first + k] = squares[k]

    def window(values):
        twos = [values[k] + values[k + 1] for k in range(len(values) - 1)]
        fours = [twos[k] + twos[k + 2] for k in range(len(twos) - 2)]
        return [fours[k] + fours[k + 4] + values[k + 8] for k in range(CHUNK)]

    def share(chunk, other):
        return pltpu.make_async_remote_copy(
            src_ref=attr.at[pl.ds(chunk * CHUNK, CHUNK)],
            dst_ref=base.at[pl.ds(HALF + chunk * CHUNK, CHUNK)],
            send_sem=base_send.at[chunk, other - 1],
            recv_sem=base_recv.at[chunk],
            device_id={"vintage": other},
            device_id_type=MESH,
        )

    @pl.loop(0, CHUNKS)
    def _(chunk):
        first = chunk * CHUNK
        sums = [stack[first + k] for k in range(CHUNK + 2 * RT)]
        numer = window([s * s for s in sums])
        denom = window([power[first + k] for k in range(CHUNK + 2 * RT)])
        for k in range(CHUNK):
            semb = numer[k] / (9.0 * denom[k] + EPS)
            semb_t[pl.ds(first + k, NWIN, stride=WIN), :] = semb
            attr[first + k] = semb * sums[RT + k] * (1.0 / 9.0)

        @pl.when(v == 0)
        def _():
            for other in range(1, vintages):
                share(chunk, other).start()

    semb_n[...] = semb_t[...].T
    semb_store = pltpu.make_async_copy(semb_n, semb_out, store_sem.at[0])
    semb_store.start()

    def energy(ref, first):
        parts = [ref[first + k] * ref[first + k] for k in range(WIN)]
        while len(parts) > 1:
            parts = [parts[k] + parts[k + 1] for k in range(0, len(parts), 2)]
        return jnp.sum(parts[0], axis=0, keepdims=True)

    mon_energy = energy(attr, 0)

    @pl.when(v == 0)
    def _():
        base[HALF : HALF + WIN] = attr[...]

    @pl.when(v != 0)
    def _():
        for chunk in range(CHUNKS):
            share(chunk, 1).wait_recv()

    base_energy = energy(base, HALF)
    win = lax.broadcasted_iota(jnp.int32, (NWIN, lanes), 0)
    for k in range(HALF):
        base[k] = jnp.where(win == 0, 0.0, pltpu.roll(base[k + WIN], 1, 0))
        base[k + HALF + WIN] = jnp.where(win == NWIN - 1, 0.0, pltpu.roll(base[k + HALF], NWIN - 1, 0))

    def add_chunk(chunk, acc):
        first = chunk * CHUNK
        mine = [attr[first + k] for k in range(CHUNK)]
        acc = list(acc)
        for j in range(CHUNK + LAGS - 1):
            other = base[first + j]
            for k in range(CHUNK):
                if 0 <= j - k < LAGS:
                    acc[j - k] = acc[j - k] + mine[k] * other
        return tuple(acc)

    zero = jnp.zeros((NWIN, lanes), jnp.float32)
    acc = lax.fori_loop(0, CHUNKS, add_chunk, (zero,) * LAGS)
    factor = jnp.broadcast_to(NWIN / jnp.sqrt(mon_energy * base_energy + EPS), (NWIN, lanes))
    for lag in range(LAGS):
        corr_t[lag * NWIN : (lag + 1) * NWIN, :] = acc[lag] * factor
    corr_n[:, 0:TIME_SAMPLES] = corr_t[0:TIME_SAMPLES, :].T
    corr_n[:, TIME_SAMPLES : LAGS * NWIN] = corr_t[TIME_SAMPLES : LAGS * NWIN, :].T
    corr_store = pltpu.make_async_copy(corr_n, corr_out, store_sem.at[1])
    corr_store.start()

    for index, (a, b) in enumerate(DIRECTIONS):

        @pl.when(inside(a, b))
        def _():
            halo(index).wait_send()

    @pl.when(v == 0)
    def _():
        for chunk in range(CHUNKS):
            for other in range(1, vintages):
                share(chunk, other).wait_send()

    semb_store.wait()
    corr_store.wait()


def per_device(vintages, inlines, xlines, amplitude, inline_slope, crossline_slope):
    _, rows, cols, _ = amplitude.shape
    lanes = rows * cols
    f32 = jnp.float32
    anywhere = pl.BlockSpec(memory_space=pl.ANY)
    semb, correl = pl.pallas_call(
        functools.partial(kernel, rows, cols, vintages, inlines, xlines),
        out_shape=(
            jax.ShapeDtypeStruct((lanes, TIME_SAMPLES), f32),
            jax.ShapeDtypeStruct((lanes, LAGS * NWIN), f32),
        ),
        in_specs=[anywhere] * 3,
        out_specs=(anywhere, anywhere),
        scratch_shapes=[
            pltpu.VMEM((rows + 2, cols + 2 * PAD, TIME_SAMPLES), f32),
            pltpu.VMEM((len(OFFSETS), TIME_SAMPLES + 2 * PAD, lanes), f32),
            pltpu.VMEM((WIN + 2 * RT, NWIN, lanes), f32),
            pltpu.VMEM((WIN + 2 * RT, NWIN, lanes), f32),
            pltpu.VMEM((WIN, NWIN, lanes), f32),
            pltpu.VMEM((WIN + 2 * HALF, NWIN, lanes), f32),
            pltpu.VMEM((TIME_SAMPLES, lanes), f32),
            pltpu.VMEM((lanes, TIME_SAMPLES), f32),
            pltpu.VMEM((LAGS * NWIN, lanes), f32),
            pltpu.VMEM((lanes, LAGS * NWIN), f32),
            pltpu.VMEM((rows, cols), jnp.int32),
            pltpu.VMEM((rows, cols), jnp.int32),
            pltpu.SemaphoreType.DMA((3,)),
            pltpu.SemaphoreType.DMA((2,)),
            pltpu.SemaphoreType.DMA((len(DIRECTIONS),)),
            pltpu.SemaphoreType.DMA((len(DIRECTIONS),)),
            pltpu.SemaphoreType.DMA((CHUNKS, max(vintages - 1, 1))),
            pltpu.SemaphoreType.DMA((CHUNKS,)),
        ],
        compiler_params=pltpu.CompilerParams(
            collective_id=0, has_side_effects=True, vmem_limit_bytes=16 * 2**20
        ),
        name="steer_and_correlate",
    )(amplitude, inline_slope, crossline_slope)
    return (
        semb.reshape(1, rows, cols, TIME_SAMPLES),
        correl.reshape(1, rows, cols, LAGS * NWIN),
    )


def solution(mesh):
    sizes = [mesh.shape[axis] for axis in ("vintage", "inline", "xline")]
    return jax.shard_map(
        functools.partial(per_device, *sizes),
        mesh=mesh,
        in_specs=(
            P("vintage", "inline", "xline", None),
            P("vintage", "inline", "xline"),
            P("vintage", "inline", "xline"),
        ),
        out_specs=(P("vintage", "inline", "xline", None), P("vintage", "inline", "xline", None)),
        check_vma=False,
    )
```

time: 141 us -> 18.4 us (0.13)
  the two profiles are of different devices: /device:TPU:0 before, /device:TPU:13 now
where the time goes in v1:
time: 18.4 us; the launch traced here: 18.1 us
  Pallas kernels  13.8 us (75%)
  local copies, waits for them, and re-layouts  3.6 us (20%)
  between operations  0.65 us (4%)
    pallas_call x1, Pallas kernels, per_device(): pl.pallas_call(functools.partial(kernel, rows, cols, vintages, inlines, x...  13.8 us
    unnamed x8, local copies, waits for them, and re-layouts  3.6 us

profile of v1, /device:TPU:13, one launch (start us, length us, event | category | flops | bytes accessed | tf_op | source)
XLA Modules:
  0.0 18.1 jit_solution(2428093727324887353)
XLA Ops:
  0.6 0.0 copy-start
  0.6 0.9 %copy-done = f32[1,8,16,256]{3,2,1,0:T(8,128)S(1)} copy-done((f32[1,8,16,256]{3,2,1,0:T(8,128)S(1)}, f32[1,8,16,256]{3,2,1,0:T(8,128)}, u32[]{:S(2)}) %copy-start) | copy-done | bytes 131096
  1.5 0.0 copy-start.1
  1.5 0.7 %copy-done.1 = s32[1,8,16]{2,1,0:T(8,128)S(1)} copy-done((s32[1,8,16]{2,1,0:T(8,128)S(1)}, s32[1,8,16]{2,1,0:T(8,128)}, u32[]{:S(2)}) %copy-start.1) | copy-done | bytes 536
  2.2 0.0 copy-start.2
  2.2 0.7 %copy-done.2 = s32[1,8,16]{2,1,0:T(8,128)S(1)} copy-done((s32[1,8,16]{2,1,0:T(8,128)S(1)}, s32[1,8,16]{2,1,0:T(8,128)}, u32[]{:S(2)}) %copy-start.2) | copy-done | bytes 536
  2.9 13.8 %steer_and_correlate.1 = (f32[128,256]{1,0:T(8,128)S(1)}, f32[128,264]{1,0:T(8,128)S(1)}) custom-call(f32[1,8,16,256]{3,2,1,0:T(8,128)S(1)} %copy-done, s32[1,8,16]{2,1,0:T(8,128)S(1)} %copy-done.1, s32[1,8,16]{2,1,0:T(8,128)S(1)} %copy-done.2), custom_call_target="tpu_custom_call" | custom-call | tf_op jit(solution)/shard_map/steer_and_correlate/pallas_call | solution.py:265
  16.7 0.7 %copy.7 = f32[1,8,16,256]{3,2,1,0:T(8,128)} copy(f32[1,8,16,256]{3,2,1,0:T(8,128)S(1)} %bitcast.3) | data formatting | bytes 262144
  17.4 0.7 %copy.8 = f32[1,8,16,264]{3,2,1,0:T(8,128)} copy(f32[1,8,16,264]{3,2,1,0:T(8,128)S(1)} %bitcast.2) | data formatting | bytes 270336
Async XLA Ops:
  0.6 0.9 %copy-start = (f32[1,8,16,256]{3,2,1,0:T(8,128)S(1)}, f32[1,8,16,256]{3,2,1,0:T(8,128)}, u32[]{:S(2)}) copy-start(f32[1,8,16,256]{3,2,1,0:T(8,128)} %amp.1) | copy-start | bytes 393220
  1.5 0.7 %copy-start.1 = (s32[1,8,16]{2,1,0:T(8,128)S(1)}, s32[1,8,16]{2,1,0:T(8,128)}, u32[]{:S(2)}) copy-start(s32[1,8,16]{2,1,0:T(8,128)} %dip_il.1) | copy-start | bytes 1540
  2.2 0.7 %copy-start.2 = (s32[1,8,16]{2,1,0:T(8,128)S(1)}, s32[1,8,16]{2,1,0:T(8,128)}, u32[]{:S(2)}) copy-start(s32[1,8,16]{2,1,0:T(8,128)} %dip_xl.1) | copy-start | bytes 1540

commit v2 on v1

--- a/solution.py
+++ b/solution.py
@@ -53,11 +53,11 @@
     return rows[:CHUNK]
 
 
-def kernel(
+def steer_kernel(
     rows, cols, vintages, inlines, xlines,
-    amp, dip_il, dip_xl, semb_out, corr_out,
-    tile, times, stack, power, attr, base, semb_t, semb_n, corr_t, corr_n, d_il, d_xl,
-    load_sem, store_sem, halo_send, halo_recv, base_send, base_recv,
+    amp, dip_il, dip_xl, attr, base, semb_t,
+    tile, times, d_il, d_xl,
+    load_sem, halo_send, halo_recv, base_send, base_recv,
 ):
     v = lax.axis_index("vintage")
     i = lax.axis_index("inline")
@@ -92,11 +92,15 @@
                 barrier, inc=1, device_id={"inline": i + a, "xline": x + b}, device_id_type=MESH
             )
 
+    direct = [other for other in range(1, vintages) if other == 1 or other % 2 == 0]
+    passes_on = (v % 2 == 0) & (v > 0) & (v + 1 < vintages)
+
     @pl.when(v != 0)
     def _():
-        pl.semaphore_signal(barrier, inc=1, device_id={"vintage": 0}, device_id_type=MESH)
-
-    greeted = greeted + jnp.where(v == 0, vintages - 1, 0)
+        parent = jnp.where((v % 2 == 1) & (v > 1), v - 1, 0)
+        pl.semaphore_signal(barrier, inc=1, device_id={"vintage": parent}, device_id_type=MESH)
+
+    greeted = greeted + jnp.where(v == 0, len(direct), 0) + jnp.where(passes_on, 1, 0)
     pl.semaphore_wait(barrier, greeted)
 
     def halo(index):
@@ -140,8 +144,7 @@
         block = tile[1 + a : 1 + a + rows, PAD + b : PAD + b + cols, :]
         times[slot, PAD : PAD + TIME_SAMPLES, :] = block.reshape(lanes, TIME_SAMPLES).T
 
-    @pl.loop(0, CHUNKS + 1)
-    def _(chunk):
+    def stack_chunk(chunk):
         first = chunk * CHUNK
         total = [None] * CHUNK
         squares = [None] * CHUNK
@@ -158,9 +161,7 @@
                 square = moved[k] * moved[k]
                 total[k] = moved[k] if total[k] is None else total[k] + moved[k]
                 squares[k] = square if squares[k] is None else squares[k] + square
-        for k in range(CHUNK):
-            stack[first + k] = total[k]
-            power[first + k] = squares[k]
+        return total, squares
 
     def window(values):
         twos = [values[k] + values[k + 1] for k in range(len(values) - 1)]
@@ -170,19 +171,29 @@
     def share(chunk, other):
         return pltpu.make_async_remote_copy(
             src_ref=attr.at[pl.ds(chunk * CHUNK, CHUNK)],
-            dst_ref=base.at[pl.ds(HALF + chunk * CHUNK, CHUNK)],
-            send_sem=base_send.at[chunk, other - 1],
+            dst_ref=base.at[pl.ds(chunk * CHUNK, CHUNK)],
+            send_sem=base_send.at[chunk, direct.index(other)],
             recv_sem=base_recv.at[chunk],
             device_id={"vintage": other},
             device_id_type=MESH,
         )
 
-    @pl.loop(0, CHUNKS)
-    def _(chunk):
+    def pass_on(chunk):
+        return pltpu.make_async_remote_copy(
+            src_ref=base.at[pl.ds(chunk * CHUNK, CHUNK)],
+            dst_ref=base.at[pl.ds(chunk * CHUNK, CHUNK)],
+            send_sem=base_send.at[chunk, 0],
+            recv_sem=base_recv.at[chunk],
+            device_id={"vintage": v + 1},
+            device_id_type=MESH,
+        )
+
+    def attribute_chunk(chunk, carried):
+        total, squares = stack_chunk(chunk + 1)
         first = chunk * CHUNK
-        sums = [stack[first + k] for k in range(CHUNK + 2 * RT)]
+        sums = list(carried[0]) + total
         numer = window([s * s for s in sums])
-        denom = window([power[first + k] for k in range(CHUNK + 2 * RT)])
+        denom = window(list(carried[1]) + squares)
         for k in range(CHUNK):
             semb = numer[k] / (9.0 * denom[k] + EPS)
             semb_t[pl.ds(first + k, NWIN, stride=WIN), :] = semb
@@ -190,42 +201,74 @@
 
         @pl.when(v == 0)
         def _():
-            for other in range(1, vintages):
+            for other in direct:
                 share(chunk, other).start()
 
+        return total, squares
+
+    lax.fori_loop(0, CHUNKS, attribute_chunk, stack_chunk(0))
+
+    @pl.when(v == 0)
+    def _():
+        base[...] = attr[...]
+
+    @pl.when(v != 0)
+    def _():
+        for chunk in range(CHUNKS):
+            pass_on(chunk).wait_recv()
+
+            @pl.when(passes_on)
+            def _():
+                pass_on(chunk).start()
+
+    for index, (a, b) in enumerate(DIRECTIONS):
+
+        @pl.when(inside(a, b))
+        def _():
+            halo(index).wait_send()
+
+    @pl.when(v == 0)
+    def _():
+        for chunk in range(CHUNKS):
+            for other in direct:
+                share(chunk, other).wait_send()
+
+    @pl.when(passes_on)
+    def _():
+        for chunk in range(CHUNKS):
+            pass_on(chunk).wait_send()
+
+
+def correlate_kernel(
+    attr, base, semb_t, semb_out, corr_out, wide, semb_n, corr_t, corr_n, store_sem
+):
+    lanes = attr.shape[2]
     semb_n[...] = semb_t[...].T
     semb_store = pltpu.make_async_copy(semb_n, semb_out, store_sem.at[0])
     semb_store.start()
 
-    def energy(ref, first):
-        parts = [ref[first + k] * ref[first + k] for k in range(WIN)]
+    win = lax.broadcasted_iota(jnp.int32, (NWIN, lanes), 0)
+    for k in range(WIN):
+        wide[HALF + k] = base[k]
+    for k in range(HALF):
+        wide[k] = jnp.where(win == 0, 0.0, pltpu.roll(base[k + WIN - HALF], 1, 0))
+        wide[HALF + WIN + k] = jnp.where(win == NWIN - 1, 0.0, pltpu.roll(base[k], NWIN - 1, 0))
+
+    def energy(ref):
+        parts = [ref[k] * ref[k] for k in range(WIN)]
         while len(parts) > 1:
             parts = [parts[k] + parts[k + 1] for k in range(0, len(parts), 2)]
         return jnp.sum(parts[0], axis=0, keepdims=True)
 
-    mon_energy = energy(attr, 0)
-
-    @pl.when(v == 0)
-    def _():
-        base[HALF : HALF + WIN] = attr[...]
-
-    @pl.when(v != 0)
-    def _():
-        for chunk in range(CHUNKS):
-            share(chunk, 1).wait_recv()
-
-    base_energy = energy(base, HALF)
-    win = lax.broadcasted_iota(jnp.int32, (NWIN, lanes), 0)
-    for k in range(HALF):
-        base[k] = jnp.where(win == 0, 0.0, pltpu.roll(base[k + WIN], 1, 0))
-        base[k + HALF + WIN] = jnp.where(win == NWIN - 1, 0.0, pltpu.roll(base[k + HALF], NWIN - 1, 0))
+    factor = NWIN / jnp.sqrt(energy(attr) * energy(base) + EPS)
+    factor = jnp.broadcast_to(factor, (NWIN, lanes))
 
     def add_chunk(chunk, acc):
         first = chunk * CHUNK
         mine = [attr[first + k] for k in range(CHUNK)]
         acc = list(acc)
         for j in range(CHUNK + LAGS - 1):
-            other = base[first + j]
+            other = wide[first + j]
             for k in range(CHUNK):
                 if 0 <= j - k < LAGS:
                     acc[j - k] = acc[j - k] + mine[k] * other
@@ -233,26 +276,12 @@
 
     zero = jnp.zeros((NWIN, lanes), jnp.float32)
     acc = lax.fori_loop(0, CHUNKS, add_chunk, (zero,) * LAGS)
-    factor = jnp.broadcast_to(NWIN / jnp.sqrt(mon_energy * base_energy + EPS), (NWIN, lanes))
     for lag in range(LAGS):
         corr_t[lag * NWIN : (lag + 1) * NWIN, :] = acc[lag] * factor
     corr_n[:, 0:TIME_SAMPLES] = corr_t[0:TIME_SAMPLES, :].T
     corr_n[:, TIME_SAMPLES : LAGS * NWIN] = corr_t[TIME_SAMPLES : LAGS * NWIN, :].T
     corr_store = pltpu.make_async_copy(corr_n, corr_out, store_sem.at[1])
     corr_store.start()
-
-    for index, (a, b) in enumerate(DIRECTIONS):
-
-        @pl.when(inside(a, b))
-        def _():
-            halo(index).wait_send()
-
-    @pl.when(v == 0)
-    def _():
-        for chunk in range(CHUNKS):
-            for other in range(1, vintages):
-                share(chunk, other).wait_send()
-
     semb_store.wait()
     corr_store.wait()
 
@@ -261,40 +290,55 @@
     _, rows, cols, _ = amplitude.shape
     lanes = rows * cols
     f32 = jnp.float32
-    anywhere = pl.BlockSpec(memory_space=pl.ANY)
-    semb, correl = pl.pallas_call(
-        functools.partial(kernel, rows, cols, vintages, inlines, xlines),
+    in_hbm = pl.BlockSpec(memory_space=pltpu.HBM)
+    in_vmem = pl.BlockSpec(memory_space=pltpu.VMEM)
+    operands = [
+        pltpu.with_memory_space_constraint(array, pltpu.HBM)
+        for array in (amplitude, inline_slope, crossline_slope)
+    ]
+    held = pl.pallas_call(
+        functools.partial(steer_kernel, rows, cols, vintages, inlines, xlines),
         out_shape=(
-            jax.ShapeDtypeStruct((lanes, TIME_SAMPLES), f32),
-            jax.ShapeDtypeStruct((lanes, LAGS * NWIN), f32),
+            pltpu.VMEM((WIN, NWIN, lanes), f32),
+            pltpu.VMEM((WIN, NWIN, lanes), f32),
+            pltpu.VMEM((TIME_SAMPLES, lanes), f32),
         ),
-        in_specs=[anywhere] * 3,
-        out_specs=(anywhere, anywhere),
+        in_specs=[in_hbm] * 3,
+        out_specs=(in_vmem,) * 3,
         scratch_shapes=[
             pltpu.VMEM((rows + 2, cols + 2 * PAD, TIME_SAMPLES), f32),
             pltpu.VMEM((len(OFFSETS), TIME_SAMPLES + 2 * PAD, lanes), f32),
-            pltpu.VMEM((WIN + 2 * RT, NWIN, lanes), f32),
-            pltpu.VMEM((WIN + 2 * RT, NWIN, lanes), f32),
-            pltpu.VMEM((WIN, NWIN, lanes), f32),
-            pltpu.VMEM((WIN + 2 * HALF, NWIN, lanes), f32),
-            pltpu.VMEM((TIME_SAMPLES, lanes), f32),
-            pltpu.VMEM((lanes, TIME_SAMPLES), f32),
-            pltpu.VMEM((LAGS * NWIN, lanes), f32),
-            pltpu.VMEM((lanes, LAGS * NWIN), f32),
             pltpu.VMEM((rows, cols), jnp.int32),
             pltpu.VMEM((rows, cols), jnp.int32),
             pltpu.SemaphoreType.DMA((3,)),
-            pltpu.SemaphoreType.DMA((2,)),
             pltpu.SemaphoreType.DMA((len(DIRECTIONS),)),
             pltpu.SemaphoreType.DMA((len(DIRECTIONS),)),
-            pltpu.SemaphoreType.DMA((CHUNKS, max(vintages - 1, 1))),
+            pltpu.SemaphoreType.DMA((CHUNKS, max(vintages // 2 + 1, 1))),
             pltpu.SemaphoreType.DMA((CHUNKS,)),
         ],
         compiler_params=pltpu.CompilerParams(
             collective_id=0, has_side_effects=True, vmem_limit_bytes=16 * 2**20
         ),
-        name="steer_and_correlate",
-    )(amplitude, inline_slope, crossline_slope)
+        name="steer",
+    )(*operands)
+    semb, correl = pl.pallas_call(
+        correlate_kernel,
+        out_shape=(
+            pltpu.HBM((lanes, TIME_SAMPLES), f32),
+            pltpu.HBM((lanes, LAGS * NWIN), f32),
+        ),
+        in_specs=[in_vmem] * 3,
+        out_specs=(in_hbm, in_hbm),
+        scratch_shapes=[
+            pltpu.VMEM((WIN + 2 * HALF, NWIN, lanes), f32),
+            pltpu.VMEM((lanes, TIME_SAMPLES), f32),
+            pltpu.VMEM((LAGS * NWIN, lanes), f32),
+            pltpu.VMEM((lanes, LAGS * NWIN), f32),
+            pltpu.SemaphoreType.DMA((2,)),
+        ],
+        compiler_params=pltpu.CompilerParams(vmem_limit_bytes=16 * 2**20),
+        name="correlate",
+    )(*[pltpu.with_memory_space_constraint(array, pltpu.VMEM) for array in held])
     return (
         semb.reshape(1, rows, cols, TIME_SAMPLES),
         correl.reshape(1, rows, cols, LAGS * NWIN),

time: 18.4 us -> 14.2 us (0.77)
  local copies, waits for them, and re-layouts: 3.6 us -> 0 us
  Pallas kernels: 13.8 us -> 13.4 us
    unnamed x8 -> x0, local copies, waits for them, and re-layouts: 3.6 us -> none
    pallas_call x1 -> x2, Pallas kernels: 13.8 us -> 13.4 us  [the longest x1 12.1 us: per_device(): pl.pallas_call(functools.partial(steer_kernel, rows, cols, vintages, inli...]
where the time goes in v2:
time: 14.2 us; the launch traced here: 14 us
  Pallas kernels  13.4 us (94%)
  between operations  0.64 us (5%)
    pallas_call x1, Pallas kernels, per_device(): pl.pallas_call(functools.partial(steer_kernel, rows, cols, vintages, inli...  12.1 us
    pallas_call x1, Pallas kernels, per_device(): pl.pallas_call(correlate_kernel, out_shape=(pltpu.HBM((lanes, TIME_SAMPLE...  1.25 us

profile of v2, /device:TPU:13, one launch (start us, length us, event | category | flops | bytes accessed | tf_op | source)
XLA Modules:
  0.0 14.0 jit_solution(15106136381356117574)
XLA Ops:
  0.6 12.1 %steer.1 = (f32[32,8,128]{2,1,0:T(8,128)S(1)}, f32[32,8,128]{2,1,0:T(8,128)S(1)}, f32[256,128]{1,0:T(8,128)S(1)}) custom-call(f32[1,8,16,256]{3,2,1,0:T(8,128)} %amp.1, s32[1,8,16]{2,1,0:T(8,128)} %dip_il.1, s32[1,8,16]{2,1,0:T(8,128)} %dip_xl.1), custom_call_target="tpu_custom_call" | custom-call | tf_op jit(solution)/shard_map/steer/pallas_call | solution.py:299
  12.8 1.2 %correlate.1 = (f32[128,256]{1,0:T(8,128)}, f32[128,264]{1,0:T(8,128)}) custom-call(f32[32,8,128]{2,1,0:T(8,128)S(1)} %get-tuple-element.7.attr, f32[32,8,128]{2,1,0:T(8,128)S(1)} %get-tuple-element.8.base, f32[256,128]{1,0:T(8,128)S(1)} %get-tuple-element.9.semb_t), custom_call_target="tpu_custom_call" | custom-call | tf_op jit(solution)/shard_map/correlate/pallas_call | solution.py:324

commit v3 on v2

--- a/solution.py
+++ b/solution.py
@@ -21,7 +21,7 @@
 CHUNK = 8
 CHUNKS = WIN // CHUNK
 MESH = pl.DeviceIdType.MESH
-DIRECTIONS = [(a, b) for a in (-1, 0, 1) for b in (-1, 0, 1) if (a, b) != (0, 0)]
+DIRECTIONS = [(-1, -1), (-1, 1), (1, -1), (1, 1), (0, -1), (0, 1), (-1, 0), (1, 0)]
 OFFSETS = [(a, b) for a in (-1, 0, 1) for b in (-1, 0, 1)]
 
 
@@ -55,8 +55,8 @@
 
 def steer_kernel(
     rows, cols, vintages, inlines, xlines,
-    amp, dip_il, dip_xl, attr, base, semb_t,
-    tile, times, d_il, d_xl,
+    amp, dip_il, dip_xl, attr, base, semb_n,
+    tile, times, semb_t, d_il, d_xl,
     load_sem, halo_send, halo_recv, base_send, base_recv,
 ):
     v = lax.axis_index("vintage")
@@ -107,8 +107,8 @@
         a, b = DIRECTIONS[index]
         row_from = {-1: pl.ds(0, 1), 0: pl.ds(0, rows), 1: pl.ds(rows - 1, 1)}[a]
         row_to = {-1: pl.ds(rows + 1, 1), 0: pl.ds(1, rows), 1: pl.ds(0, 1)}[a]
-        col_from = {-1: pl.ds(0, PAD), 0: pl.ds(0, cols), 1: pl.ds(cols - PAD, PAD)}[b]
-        col_to = {-1: pl.ds(PAD + cols, PAD), 0: pl.ds(PAD, cols), 1: pl.ds(0, PAD)}[b]
+        col_from = {-1: pl.ds(0, 1), 0: pl.ds(0, cols), 1: pl.ds(cols - 1, 1)}[b]
+        col_to = {-1: pl.ds(PAD + cols, 1), 0: pl.ds(PAD, cols), 1: pl.ds(PAD - 1, 1)}[b]
         return pltpu.make_async_remote_copy(
             src_ref=amp.at[0, row_from, col_from, :],
             dst_ref=tile.at[row_to, col_to, :],
@@ -134,15 +134,20 @@
         times[slot, 0:PAD, :] = blank
         times[slot, PAD + TIME_SAMPLES : 2 * PAD + TIME_SAMPLES, :] = blank
 
-    for index, (a, b) in enumerate(DIRECTIONS):
+    def turn(a, b):
+        block = tile[1 + a : 1 + a + rows, PAD + b : PAD + b + cols, :]
+        slot = OFFSETS.index((a, b))
+        times[slot, PAD : PAD + TIME_SAMPLES, :] = block.reshape(lanes, TIME_SAMPLES).T
+
+    turn(0, 0)
+    for index in range(len(DIRECTIONS) - 1, -1, -1):
+        a, b = DIRECTIONS[index]
 
         @pl.when(inside(-a, -b))
         def _():
             halo(index).wait_recv()
 
-    for slot, (a, b) in enumerate(OFFSETS):
-        block = tile[1 + a : 1 + a + rows, PAD + b : PAD + b + cols, :]
-        times[slot, PAD : PAD + TIME_SAMPLES, :] = block.reshape(lanes, TIME_SAMPLES).T
+        turn(-a, -b)
 
     def stack_chunk(chunk):
         first = chunk * CHUNK
@@ -208,6 +213,8 @@
 
     lax.fori_loop(0, CHUNKS, attribute_chunk, stack_chunk(0))
 
+    semb_n[...] = semb_t[...].T
+
     @pl.when(v == 0)
     def _():
         base[...] = attr[...]
@@ -240,10 +247,9 @@
 
 
 def correlate_kernel(
-    attr, base, semb_t, semb_out, corr_out, wide, semb_n, corr_t, corr_n, store_sem
+    attr, base, semb_n, semb_out, corr_out, wide, corr_t, corr_n, store_sem
 ):
     lanes = attr.shape[2]
-    semb_n[...] = semb_t[...].T
     semb_store = pltpu.make_async_copy(semb_n, semb_out, store_sem.at[0])
     semb_store.start()
 
@@ -301,13 +307,14 @@
         out_shape=(
             pltpu.VMEM((WIN, NWIN, lanes), f32),
             pltpu.VMEM((WIN, NWIN, lanes), f32),
-            pltpu.VMEM((TIME_SAMPLES, lanes), f32),
+            pltpu.VMEM((lanes, TIME_SAMPLES), f32),
         ),
         in_specs=[in_hbm] * 3,
         out_specs=(in_vmem,) * 3,
         scratch_shapes=[
             pltpu.VMEM((rows + 2, cols + 2 * PAD, TIME_SAMPLES), f32),
             pltpu.VMEM((len(OFFSETS), TIME_SAMPLES + 2 * PAD, lanes), f32),
+            pltpu.VMEM((TIME_SAMPLES, lanes), f32),
             pltpu.VMEM((rows, cols), jnp.int32),
             pltpu.VMEM((rows, cols), jnp.int32),
             pltpu.SemaphoreType.DMA((3,)),
@@ -331,7 +338,6 @@
         out_specs=(in_hbm, in_hbm),
         scratch_shapes=[
             pltpu.VMEM((WIN + 2 * HALF, NWIN, lanes), f32),
-            pltpu.VMEM((lanes, TIME_SAMPLES), f32),
             pltpu.VMEM((LAGS * NWIN, lanes), f32),
             pltpu.VMEM((lanes, LAGS * NWIN), f32),
             pltpu.SemaphoreType.DMA((2,)),

time: 14.2 us -> 14.7 us (1.035)
  Pallas kernels: 13.4 us -> 13.9 us
    pallas_call x1, Pallas kernels: 12.1 us -> 12.7 us  [per_device(): pl.pallas_call(functools.partial(steer_kernel, rows, cols, vintages, inli...]
where the time goes in v3:
time: 14.7 us; the launch traced here: 14.5 us
  Pallas kernels  13.9 us (95%)
  between operations  0.64 us (4%)
    pallas_call x1, Pallas kernels, per_device(): pl.pallas_call(functools.partial(steer_kernel, rows, cols, vintages, inli...  12.7 us
    pallas_call x1, Pallas kernels, per_device(): pl.pallas_call(correlate_kernel, out_shape=(pltpu.HBM((lanes, TIME_SAMPLE...  1.2 us

profile of v3, /device:TPU:13, one launch (start us, length us, event | category | flops | bytes accessed | tf_op | source)
XLA Modules:
  0.0 14.5 jit_solution(17806956849289374217)
XLA Ops:
  0.6 12.7 %steer.1 = (f32[32,8,128]{2,1,0:T(8,128)S(1)}, f32[32,8,128]{2,1,0:T(8,128)S(1)}, f32[128,256]{1,0:T(8,128)S(1)}) custom-call(f32[1,8,16,256]{3,2,1,0:T(8,128)} %amp.1, s32[1,8,16]{2,1,0:T(8,128)} %dip_il.1, s32[1,8,16]{2,1,0:T(8,128)} %dip_xl.1), custom_call_target="tpu_custom_call" | custom-call | tf_op jit(solution)/shard_map/steer/pallas_call | solution.py:305
  13.3 1.2 %correlate.1 = (f32[128,256]{1,0:T(8,128)}, f32[128,264]{1,0:T(8,128)}) custom-call(f32[32,8,128]{2,1,0:T(8,128)S(1)} %get-tuple-element.7.attr, f32[32,8,128]{2,1,0:T(8,128)S(1)} %get-tuple-element.8.base, f32[128,256]{1,0:T(8,128)S(1)} %get-tuple-element.9.semb_n), custom_call_target="tpu_custom_call" | custom-call | tf_op jit(solution)/shard_map/correlate/pallas_call | solution.py:331

commit v4 on v3

--- a/solution.py
+++ b/solution.py
@@ -56,7 +56,7 @@
 def steer_kernel(
     rows, cols, vintages, inlines, xlines,
     amp, dip_il, dip_xl, attr, base, semb_n,
-    tile, times, semb_t, d_il, d_xl,
+    tile, times, rows_of, semb_t, d_il, d_xl,
     load_sem, halo_send, halo_recv, base_send, base_recv,
 ):
     v = lax.axis_index("vintage")
@@ -107,8 +107,8 @@
         a, b = DIRECTIONS[index]
         row_from = {-1: pl.ds(0, 1), 0: pl.ds(0, rows), 1: pl.ds(rows - 1, 1)}[a]
         row_to = {-1: pl.ds(rows + 1, 1), 0: pl.ds(1, rows), 1: pl.ds(0, 1)}[a]
-        col_from = {-1: pl.ds(0, 1), 0: pl.ds(0, cols), 1: pl.ds(cols - 1, 1)}[b]
-        col_to = {-1: pl.ds(PAD + cols, 1), 0: pl.ds(PAD, cols), 1: pl.ds(PAD - 1, 1)}[b]
+        col_from = {-1: pl.ds(0, PAD), 0: pl.ds(0, cols), 1: pl.ds(cols - PAD, PAD)}[b]
+        col_to = {-1: pl.ds(PAD + cols, PAD), 0: pl.ds(PAD, cols), 1: pl.ds(0, PAD)}[b]
         return pltpu.make_async_remote_copy(
             src_ref=amp.at[0, row_from, col_from, :],
             dst_ref=tile.at[row_to, col_to, :],
@@ -129,15 +129,20 @@
     dips = [lane_dips(d_il[...], rows, cols), lane_dips(d_xl[...], rows, cols)]
     lanes = rows * cols
     dips = [jnp.broadcast_to(dip, (NWIN, lanes)) for dip in dips]
-    blank = jnp.zeros((PAD, lanes), jnp.float32)
-    for slot in range(len(OFFSETS)):
-        times[slot, 0:PAD, :] = blank
-        times[slot, PAD + TIME_SAMPLES : 2 * PAD + TIME_SAMPLES, :] = blank
+    win = lax.broadcasted_iota(jnp.int32, (NWIN, lanes), 0)
 
     def turn(a, b):
         block = tile[1 + a : 1 + a + rows, PAD + b : PAD + b + cols, :]
         slot = OFFSETS.index((a, b))
-        times[slot, PAD : PAD + TIME_SAMPLES, :] = block.reshape(lanes, TIME_SAMPLES).T
+        times[slot] = block.reshape(lanes, TIME_SAMPLES).T
+        for r in range(WIN):
+            taken = times[slot, pl.ds(r, NWIN, stride=WIN), :]
+            rows_of[slot, PAD + r] = taken
+            if r < PAD:
+                later = jnp.where(win == NWIN - 1, 0.0, pltpu.roll(taken, NWIN - 1, 0))
+                rows_of[slot, PAD + WIN + r] = later
+            if r >= WIN - PAD:
+                rows_of[slot, PAD + r - WIN] = jnp.where(win == 0, 0.0, pltpu.roll(taken, 1, 0))
 
     turn(0, 0)
     for index in range(len(DIRECTIONS) - 1, -1, -1):
@@ -156,7 +161,7 @@
         for slot, (a, b) in enumerate(OFFSETS):
             reach = (abs(a) + abs(b)) * MAX_DIP_STEP
             taps = [
-                times[slot, pl.ds(first + REACH - reach + k, NWIN, stride=WIN), :]
+                rows_of[slot, first + REACH - reach + k]
                 for k in range(CHUNK + 2 * reach)
             ]
             moved = taps
@@ -313,7 +318,8 @@
         out_specs=(in_vmem,) * 3,
         scratch_shapes=[
             pltpu.VMEM((rows + 2, cols + 2 * PAD, TIME_SAMPLES), f32),
-            pltpu.VMEM((len(OFFSETS), TIME_SAMPLES + 2 * PAD, lanes), f32),
+            pltpu.VMEM((len(OFFSETS), TIME_SAMPLES, lanes), f32),
+            pltpu.VMEM((len(OFFSETS), WIN + 2 * PAD, NWIN, lanes), f32),
             pltpu.VMEM((TIME_SAMPLES, lanes), f32),
             pltpu.VMEM((rows, cols), jnp.int32),
             pltpu.VMEM((rows, cols), jnp.int32),

time: 14.7 us -> 14.6 us (level)
  no operation moved by 1% of the time
where the time goes in v4:
time: 14.6 us; the launch traced here: 14.5 us
  Pallas kernels  13.8 us (95%)
  between operations  0.64 us (4%)
    pallas_call x1, Pallas kernels, per_device(): pl.pallas_call(functools.partial(steer_kernel, rows, cols, vintages, inli...  12.6 us
    pallas_call x1, Pallas kernels, per_device(): pl.pallas_call(correlate_kernel, out_shape=(pltpu.HBM((lanes, TIME_SAMPLE...  1.2 us

profile of v4, /device:TPU:13, one launch (start us, length us, event | category | flops | bytes accessed | tf_op | source)
XLA Modules:
  0.0 14.5 jit_solution(14931068703990151878)
XLA Ops:
  0.6 12.6 %steer.1 = (f32[32,8,128]{2,1,0:T(8,128)S(1)}, f32[32,8,128]{2,1,0:T(8,128)S(1)}, f32[128,256]{1,0:T(8,128)S(1)}) custom-call(f32[1,8,16,256]{3,2,1,0:T(8,128)} %amp.1, s32[1,8,16]{2,1,0:T(8,128)} %dip_il.1, s32[1,8,16]{2,1,0:T(8,128)} %dip_xl.1), custom_call_target="tpu_custom_call" | custom-call | tf_op jit(solution)/shard_map/steer/pallas_call | solution.py:310
  13.3 1.2 %correlate.1 = (f32[128,256]{1,0:T(8,128)}, f32[128,264]{1,0:T(8,128)}) custom-call(f32[32,8,128]{2,1,0:T(8,128)S(1)} %get-tuple-element.7.attr, f32[32,8,128]{2,1,0:T(8,128)S(1)} %get-tuple-element.8.base, f32[128,256]{1,0:T(8,128)S(1)} %get-tuple-element.9.semb_n), custom_call_target="tpu_custom_call" | custom-call | tf_op jit(solution)/shard_map/correlate/pallas_call | solution.py:337

commit v5 on v4

--- a/solution.py
+++ b/solution.py
@@ -55,8 +55,8 @@
 
 def steer_kernel(
     rows, cols, vintages, inlines, xlines,
-    amp, dip_il, dip_xl, attr, base, semb_n,
-    tile, times, rows_of, semb_t, d_il, d_xl,
+    amp, dip_il, dip_xl, semb_n, corr_n,
+    tile, times, rows_of, semb_t, attr, base, corr_t, d_il, d_xl,
     load_sem, halo_send, halo_recv, base_send, base_recv,
 ):
     v = lax.axis_index("vintage")
@@ -211,7 +211,7 @@
 
         @pl.when(v == 0)
         def _():
-            for other in direct:
+            for other in reversed(direct):
                 share(chunk, other).start()
 
         return total, squares
@@ -224,14 +224,45 @@
     def _():
         base[...] = attr[...]
 
-    @pl.when(v != 0)
-    def _():
-        for chunk in range(CHUNKS):
+    def energy(ref):
+        parts = [ref[k] * ref[k] for k in range(WIN)]
+        while len(parts) > 1:
+            parts = [parts[k] + parts[k + 1] for k in range(0, len(parts), 2)]
+        return jnp.sum(parts[0], axis=0, keepdims=True)
+
+    mon_energy = energy(attr)
+
+    acc = [jnp.zeros((NWIN, lanes), jnp.float32)] * LAGS
+    for chunk in range(CHUNKS):
+
+        @pl.when(v != 0)
+        def _():
             pass_on(chunk).wait_recv()
 
             @pl.when(passes_on)
             def _():
                 pass_on(chunk).start()
+
+        placed = []
+        for r in range(chunk * CHUNK, (chunk + 1) * CHUNK):
+            row = base[r]
+            placed.append((HALF + r, row))
+            if r < HALF:
+                later = jnp.where(win == NWIN - 1, 0.0, pltpu.roll(row, NWIN - 1, 0))
+                placed.append((HALF + WIN + r, later))
+            if r >= WIN - HALF:
+                earlier = jnp.where(win == 0, 0.0, pltpu.roll(row, 1, 0))
+                placed.append((HALF + r - WIN, earlier))
+        for lag in range(LAGS):
+            for place, row in placed:
+                if 0 <= place - lag < WIN:
+                    acc[lag] = acc[lag] + attr[place - lag] * row
+
+    factor = jnp.broadcast_to(NWIN / jnp.sqrt(mon_energy * energy(base) + EPS), (NWIN, lanes))
+    for lag in range(LAGS):
+        corr_t[lag * NWIN : (lag + 1) * NWIN, :] = acc[lag] * factor
+    corr_n[:, 0:TIME_SAMPLES] = corr_t[0:TIME_SAMPLES, :].T
+    corr_n[:, TIME_SAMPLES : LAGS * NWIN] = corr_t[TIME_SAMPLES : LAGS * NWIN, :].T
 
     for index, (a, b) in enumerate(DIRECTIONS):
 
@@ -251,50 +282,15 @@
             pass_on(chunk).wait_send()
 
 
-def correlate_kernel(
-    attr, base, semb_n, semb_out, corr_out, wide, corr_t, corr_n, store_sem
-):
-    lanes = attr.shape[2]
-    semb_store = pltpu.make_async_copy(semb_n, semb_out, store_sem.at[0])
-    semb_store.start()
-
-    win = lax.broadcasted_iota(jnp.int32, (NWIN, lanes), 0)
-    for k in range(WIN):
-        wide[HALF + k] = base[k]
-    for k in range(HALF):
-        wide[k] = jnp.where(win == 0, 0.0, pltpu.roll(base[k + WIN - HALF], 1, 0))
-        wide[HALF + WIN + k] = jnp.where(win == NWIN - 1, 0.0, pltpu.roll(base[k], NWIN - 1, 0))
-
-    def energy(ref):
-        parts = [ref[k] * ref[k] for k in range(WIN)]
-        while len(parts) > 1:
-            parts = [parts[k] + parts[k + 1] for k in range(0, len(parts), 2)]
-        return jnp.sum(parts[0], axis=0, keepdims=True)
-
-    factor = NWIN / jnp.sqrt(energy(attr) * energy(base) + EPS)
-    factor = jnp.broadcast_to(factor, (NWIN, lanes))
-
-    def add_chunk(chunk, acc):
-        first = chunk * CHUNK
-        mine = [attr[first + k] for k in range(CHUNK)]
-        acc = list(acc)
-        for j in range(CHUNK + LAGS - 1):
-            other = wide[first + j]
-            for k in range(CHUNK):
-                if 0 <= j - k < LAGS:
-                    acc[j - k] = acc[j - k] + mine[k] * other
-        return tuple(acc)
-
-    zero = jnp.zeros((NWIN, lanes), jnp.float32)
-    acc = lax.fori_loop(0, CHUNKS, add_chunk, (zero,) * LAGS)
-    for lag in range(LAGS):
-        corr_t[lag * NWIN : (lag + 1) * NWIN, :] = acc[lag] * factor
-    corr_n[:, 0:TIME_SAMPLES] = corr_t[0:TIME_SAMPLES, :].T
-    corr_n[:, TIME_SAMPLES : LAGS * NWIN] = corr_t[TIME_SAMPLES : LAGS * NWIN, :].T
-    corr_store = pltpu.make_async_copy(corr_n, corr_out, store_sem.at[1])
-    corr_store.start()
-    semb_store.wait()
-    corr_store.wait()
+def store_kernel(semb_n, corr_n, semb_out, corr_out, store_sem):
+    stores = [
+        pltpu.make_async_copy(semb_n, semb_out, store_sem.at[0]),
+        pltpu.make_async_copy(corr_n, corr_out, store_sem.at[1]),
+    ]
+    for store in stores:
+        store.start()
+    for store in stores:
+        store.wait()
 
 
 def per_device(vintages, inlines, xlines, amplitude, inline_slope, crossline_slope):
@@ -310,17 +306,19 @@
     held = pl.pallas_call(
         functools.partial(steer_kernel, rows, cols, vintages, inlines, xlines),
         out_shape=(
-            pltpu.VMEM((WIN, NWIN, lanes), f32),
-            pltpu.VMEM((WIN, NWIN, lanes), f32),
             pltpu.VMEM((lanes, TIME_SAMPLES), f32),
+            pltpu.VMEM((lanes, LAGS * NWIN), f32),
         ),
         in_specs=[in_hbm] * 3,
-        out_specs=(in_vmem,) * 3,
+        out_specs=(in_vmem,) * 2,
         scratch_shapes=[
             pltpu.VMEM((rows + 2, cols + 2 * PAD, TIME_SAMPLES), f32),
             pltpu.VMEM((len(OFFSETS), TIME_SAMPLES, lanes), f32),
             pltpu.VMEM((len(OFFSETS), WIN + 2 * PAD, NWIN, lanes), f32),
             pltpu.VMEM((TIME_SAMPLES, lanes), f32),
+            pltpu.VMEM((WIN, NWIN, lanes), f32),
+            pltpu.VMEM((WIN, NWIN, lanes), f32),
+            pltpu.VMEM((LAGS * NWIN, lanes), f32),
             pltpu.VMEM((rows, cols), jnp.int32),
             pltpu.VMEM((rows, cols), jnp.int32),
             pltpu.SemaphoreType.DMA((3,)),
@@ -335,21 +333,18 @@
         name="steer",
     )(*operands)
     semb, correl = pl.pallas_call(
-        correlate_kernel,
+        store_kernel,
         out_shape=(
             pltpu.HBM((lanes, TIME_SAMPLES), f32),
             pltpu.HBM((lanes, LAGS * NWIN), f32),
         ),
-        in_specs=[in_vmem] * 3,
+        in_specs=[in_vmem] * 2,
         out_specs=(in_hbm, in_hbm),
         scratch_shapes=[
-            pltpu.VMEM((WIN + 2 * HALF, NWIN, lanes), f32),
-            pltpu.VMEM((LAGS * NWIN, lanes), f32),
-            pltpu.VMEM((lanes, LAGS * NWIN), f32),
             pltpu.SemaphoreType.DMA((2,)),
         ],
         compiler_params=pltpu.CompilerParams(vmem_limit_bytes=16 * 2**20),
-        name="correlate",
+        name="store",
     )(*[pltpu.with_memory_space_constraint(array, pltpu.VMEM) for array in held])
     return (
         semb.reshape(1, rows, cols, TIME_SAMPLES),

time: 14.6 us -> 14.4 us (0.986)
  Pallas kernels: 13.8 us -> 13.6 us
    pallas_call x1, Pallas kernels: 1.2 us -> 0.74 us  [per_device(): pl.pallas_call(store_kernel, out_shape=(pltpu.HBM((lanes, TIME_SAMPLES),...]
    pallas_call x1, Pallas kernels: 12.6 us -> 12.8 us  [per_device(): pl.pallas_call(functools.partial(steer_kernel, rows, cols, vintages, inli...]
where the time goes in v5:
time: 14.4 us; the launch traced here: 14.2 us
  Pallas kernels  13.6 us (94%)
  between operations  0.64 us (4%)
    pallas_call x1, Pallas kernels, per_device(): pl.pallas_call(functools.partial(steer_kernel, rows, cols, vintages, inli...  12.8 us
    pallas_call x1, Pallas kernels, per_device(): pl.pallas_call(store_kernel, out_shape=(pltpu.HBM((lanes, TIME_SAMPLES),...  0.74 us

profile of v5, /device:TPU:13, one launch (start us, length us, event | category | flops | bytes accessed | tf_op | source)
XLA Modules:
  0.0 14.2 jit_solution(17379347293585235758)
XLA Ops:
  0.6 12.8 %steer.1 = (f32[128,256]{1,0:T(8,128)S(1)}, f32[128,264]{1,0:T(8,128)S(1)}) custom-call(f32[1,8,16,256]{3,2,1,0:T(8,128)} %amp.1, s32[1,8,16]{2,1,0:T(8,128)} %dip_il.1, s32[1,8,16]{2,1,0:T(8,128)} %dip_xl.1), custom_call_target="tpu_custom_call" | custom-call | tf_op jit(solution)/shard_map/steer/pallas_call | solution.py:306
  13.5 0.7 %store.1 = (f32[128,256]{1,0:T(8,128)}, f32[128,264]{1,0:T(8,128)}) custom-call(f32[128,256]{1,0:T(8,128)S(1)} %get-tuple-element.6.semb_n, f32[128,264]{1,0:T(8,128)S(1)} %get-tuple-element.7.corr_n), custom_call_target="tpu_custom_call" | custom-call | tf_op jit(solution)/shard_map/store/pallas_call | solution.py:335

commit v6 on v5

--- a/solution.py
+++ b/solution.py
@@ -21,7 +21,8 @@
 CHUNK = 8
 CHUNKS = WIN // CHUNK
 MESH = pl.DeviceIdType.MESH
-DIRECTIONS = [(-1, -1), (-1, 1), (1, -1), (1, 1), (0, -1), (0, 1), (-1, 0), (1, 0)]
+DIRECTIONS = [(a, b) for a in (-1, 0, 1) for b in (-1, 0, 1) if (a, b) != (0, 0)]
+ARRIVALS = [(1, 0), (-1, 0), (0, 1), (0, -1), (1, 1), (1, -1), (-1, 1), (-1, -1)]
 OFFSETS = [(a, b) for a in (-1, 0, 1) for b in (-1, 0, 1)]
 
 
@@ -145,8 +146,8 @@
                 rows_of[slot, PAD + r - WIN] = jnp.where(win == 0, 0.0, pltpu.roll(taken, 1, 0))
 
     turn(0, 0)
-    for index in range(len(DIRECTIONS) - 1, -1, -1):
-        a, b = DIRECTIONS[index]
+    for a, b in ARRIVALS:
+        index = DIRECTIONS.index((a, b))
 
         @pl.when(inside(-a, -b))
         def _():

time: 14.4 us -> 14.3 us (level)
  no operation moved by 1% of the time
where the time goes in v6:
time: 14.3 us; the launch traced here: 14.1 us
  Pallas kernels  13.5 us (94%)
  between operations  0.64 us (4%)
    pallas_call x1, Pallas kernels, per_device(): pl.pallas_call(functools.partial(steer_kernel, rows, cols, vintages, inli...  12.8 us
    pallas_call x1, Pallas kernels, per_device(): pl.pallas_call(store_kernel, out_shape=(pltpu.HBM((lanes, TIME_SAMPLES),...  0.74 us

profile of v6, /device:TPU:13, one launch (start us, length us, event | category | flops | bytes accessed | tf_op | source)
XLA Modules:
  0.0 14.1 jit_solution(9224478607819318983)
XLA Ops:
  0.6 12.8 %steer.1 = (f32[128,256]{1,0:T(8,128)S(1)}, f32[128,264]{1,0:T(8,128)S(1)}) custom-call(f32[1,8,16,256]{3,2,1,0:T(8,128)} %amp.1, s32[1,8,16]{2,1,0:T(8,128)} %dip_il.1, s32[1,8,16]{2,1,0:T(8,128)} %dip_xl.1), custom_call_target="tpu_custom_call" | custom-call | tf_op jit(solution)/shard_map/steer/pallas_call | solution.py:307
  13.4 0.7 %store.1 = (f32[128,256]{1,0:T(8,128)}, f32[128,264]{1,0:T(8,128)}) custom-call(f32[128,256]{1,0:T(8,128)S(1)} %get-tuple-element.6.semb_n, f32[128,264]{1,0:T(8,128)S(1)} %get-tuple-element.7.corr_n), custom_call_target="tpu_custom_call" | custom-call | tf_op jit(solution)/shard_map/store/pallas_call | solution.py:336

commit v7 on v6

--- a/solution.py
+++ b/solution.py
@@ -153,6 +153,7 @@
         def _():
             halo(index).wait_recv()
 
+    for a, b in ARRIVALS:
         turn(-a, -b)
 
     def stack_chunk(chunk):

time: 14.3 us -> 14.1 us (0.986)
  Pallas kernels: 13.5 us -> 13.2 us
    pallas_call x1, Pallas kernels: 12.8 us -> 12.5 us  [per_device(): pl.pallas_call(functools.partial(steer_kernel, rows, cols, vintages, inli...]
where the time goes in v7:
time: 14.1 us; the launch traced here: 13.9 us
  Pallas kernels  13.2 us (94%)
  between operations  0.64 us (5%)
    pallas_call x1, Pallas kernels, per_device(): pl.pallas_call(functools.partial(steer_kernel, rows, cols, vintages, inli...  12.5 us
    pallas_call x1, Pallas kernels, per_device(): pl.pallas_call(store_kernel, out_shape=(pltpu.HBM((lanes, TIME_SAMPLES),...  0.74 us

profile of v7, /device:TPU:13, one launch (start us, length us, event | category | flops | bytes accessed | tf_op | source)
XLA Modules:
  0.0 13.9 jit_solution(16881311116618671119)
XLA Ops:
  0.6 12.5 %steer.1 = (f32[128,256]{1,0:T(8,128)S(1)}, f32[128,264]{1,0:T(8,128)S(1)}) custom-call(f32[1,8,16,256]{3,2,1,0:T(8,128)} %amp.1, s32[1,8,16]{2,1,0:T(8,128)} %dip_il.1, s32[1,8,16]{2,1,0:T(8,128)} %dip_xl.1), custom_call_target="tpu_custom_call" | custom-call | tf_op jit(solution)/shard_map/steer/pallas_call | solution.py:308
  13.1 0.7 %store.1 = (f32[128,256]{1,0:T(8,128)}, f32[128,264]{1,0:T(8,128)}) custom-call(f32[128,256]{1,0:T(8,128)S(1)} %get-tuple-element.6.semb_n, f32[128,264]{1,0:T(8,128)S(1)} %get-tuple-element.7.corr_n), custom_call_target="tpu_custom_call" | custom-call | tf_op jit(solution)/shard_map/store/pallas_call | solution.py:337

commit v8 on v7

--- a/solution.py
+++ b/solution.py
@@ -235,15 +235,17 @@
     mon_energy = energy(attr)
 
     acc = [jnp.zeros((NWIN, lanes), jnp.float32)] * LAGS
+    @pl.when(passes_on)
+    def _():
+        for chunk in range(CHUNKS):
+            pass_on(chunk).wait_recv()
+            pass_on(chunk).start()
+
     for chunk in range(CHUNKS):
 
-        @pl.when(v != 0)
+        @pl.when((v != 0) & jnp.logical_not(passes_on))
         def _():
             pass_on(chunk).wait_recv()
-
-            @pl.when(passes_on)
-            def _():
-                pass_on(chunk).start()
 
         placed = []
         for r in range(chunk * CHUNK, (chunk + 1) * CHUNK):

time: 14.1 us -> 14 us (level)
  no operation moved by 1% of the time
where the time goes in v8:
time: 14 us; the launch traced here: 13.8 us
  Pallas kernels  13.2 us (94%)
  between operations  0.64 us (5%)
    pallas_call x1, Pallas kernels, per_device(): pl.pallas_call(functools.partial(steer_kernel, rows, cols, vintages, inli...  12.5 us
    pallas_call x1, Pallas kernels, per_device(): pl.pallas_call(store_kernel, out_shape=(pltpu.HBM((lanes, TIME_SAMPLES),...  0.74 us

profile of v8, /device:TPU:13, one launch (start us, length us, event | category | flops | bytes accessed | tf_op | source)
XLA Modules:
  0.0 13.8 jit_solution(1351917060892620155)
XLA Ops:
  0.6 12.5 %steer.1 = (f32[128,256]{1,0:T(8,128)S(1)}, f32[128,264]{1,0:T(8,128)S(1)}) custom-call(f32[1,8,16,256]{3,2,1,0:T(8,128)} %amp.1, s32[1,8,16]{2,1,0:T(8,128)} %dip_il.1, s32[1,8,16]{2,1,0:T(8,128)} %dip_xl.1), custom_call_target="tpu_custom_call" | custom-call | tf_op jit(solution)/shard_map/steer/pallas_call | solution.py:310
  13.1 0.7 %store.1 = (f32[128,256]{1,0:T(8,128)}, f32[128,264]{1,0:T(8,128)}) custom-call(f32[128,256]{1,0:T(8,128)S(1)} %get-tuple-element.6.semb_n, f32[128,264]{1,0:T(8,128)S(1)} %get-tuple-element.7.corr_n), custom_call_target="tpu_custom_call" | custom-call | tf_op jit(solution)/shard_map/store/pallas_call | solution.py:339
